TPU v7x, 32 devices: a whole 2x2x4 slice. The times are simulated.
32 devices in a mesh: row: 4 (over y, core), col: 8 (over z, x).
Axes of the slice: x: 2, y: 2, z: 4, core: 2. Of those that a mesh axis runs over, the one named last changes fastest.
Arguments:
- transition: bfloat16 [32768, 32768], P('row', 'col'), may hold values from 1.5258789e-06 to 0.0024414062, as said below
- emission: bfloat16 [96, 32768], P(None, 'col'), may hold values from 0.0099487305 to 1
- token_ids: int32 [2, 192], replicated, may hold values from 0 to 95
- forward: bfloat16 [2, 192, 32768], P(None, 'col', 'row'), may hold values from 3.0517578e-06 to 0.0008239746, as said below
- backward_last: float32 [192, 32768], P('row', 'col'), may hold values from 0.1 to 10
Outputs:
- backward: float32 [2, 192, 32768], P(None, 'col', 'row')
- counts: float32 [32768, 1024], P('row', 'col')
Inputs may be any that keep to these rules, and one draw needn't show every extreme that they name: Positive transition weights. Positive forward weights.
All inputs are finite; a program needn't handle non-finite values.
Results may differ from a plain program's by a relative error of at most 0.00048.
Values may be sent and summed in bfloat16 or wider, within the bound.
A program may use at most 192 MiB of HBM per device.

v0:
```python
import jax
import jax.numpy as jnp
from jax import lax
from jax.sharding import PartitionSpec as P

H = 32768
N = 192
DW = 128


def spread(value, axis, source):
    kept = jnp.where(lax.axis_index(axis) == source, value, 0).astype(value.dtype)
    return lax.psum(kept, axis)


def on_device(transition, emission, token_ids, forward, backward_last):
    row_count = lax.axis_size("row")
    col_count = lax.axis_size("col")
    col_index = lax.axis_index("col")
    ratio = col_count // row_count
    local_seqs = forward.shape[1]
    block_src = transition.shape[0]
    block_dst = transition.shape[1]
    seq_total = local_seqs * col_count
    forward_all = lax.all_gather(forward, "col", axis=1, tiled=True)
    backward_next = lax.all_gather(backward_last, "row", axis=0, tiled=True)
    columns = lax.broadcasted_iota(jnp.int32, (seq_total, emission.shape[0]), 1)
    window = transition[:, :DW]
    totals = jnp.zeros((block_src, DW), jnp.float32)
    outputs = [None, None]
    for step in (1, 0):
        onehot = (token_ids[step][:, None] == columns).astype(jnp.bfloat16)
        emitted = jnp.dot(onehot, emission, preferred_element_type=jnp.float32)
        weighted_back = (emitted * backward_next).astype(jnp.bfloat16)
        partial_value = lax.dot_general(
            weighted_back, transition, (((1,), (1,)), ((), ())), preferred_element_type=jnp.float32
        )
        alpha_all = forward_all[step].astype(jnp.float32)
        summed = lax.psum(partial_value, "col")
        mine = lax.dynamic_slice_in_dim(summed, col_index * local_seqs, local_seqs, 0)
        alpha_mine = forward[step].astype(jnp.float32)
        local_norm = lax.psum(jnp.sum(alpha_mine * mine, axis=1), "row")
        normal_all = lax.all_gather(local_norm, "col", axis=0, tiled=True)
        normal_mine = lax.dynamic_slice_in_dim(normal_all, col_index * local_seqs, local_seqs, 0)
        outputs[step] = mine / normal_mine[:, None]
        scaled = (alpha_all / normal_all[:, None]).astype(jnp.bfloat16)
        totals = totals + lax.dot_general(
            scaled,
            weighted_back[:, :DW],
            (((0,), (0,)), ((), ())),
            preferred_element_type=jnp.float32,
        )
        if step == 1:
            whole = summed / normal_all[:, None]
            piece = lax.dynamic_slice_in_dim(whole, col_index % ratio * block_dst, block_dst, 1)
            backward_next = spread(piece, "row", col_index // ratio)
    counts = window.astype(jnp.float32) * totals * (H * H / N)
    return (jnp.stack(outputs), counts)


def solution(mesh):
    in_specs = (P("row", "col"), P(None, "col"), P(), P(None, "col", "row"), P("row", "col"))
    out_specs = (P(None, "col", "row"), P("row", "col"))
    return jax.shard_map(
        on_device, mesh=mesh, in_specs=in_specs, out_specs=out_specs, check_vma=False
    )
```

profile of v0, /device:TPU:0, one launch (start us, length us, event | category | flops | bytes accessed | tf_op | source)
XLA Modules:
  0.0 741.6 jit_solution(9007567216397277755)
XLA Ops:
  7.2 0.0 copy-start
  7.2 0.0 all-gather.3.cloned.1.call-start
  7.2 0.7 all-gather.3.cloned.1.call-update
  7.9 0.0 all-reduce.6.cloned.1.call-start
  8.0 0.8 fusion.17
  8.7 32.1 %all-gather.3.cloned.1.call-done = f32[192,4096]{1,0:T(8,128)} async-done(((f32[48,4096]{1,0:T(8,128)}), f32[192,4096]{1,0:T(8,128)}) %all-gather.3.cloned.1.call-update) | async-done | bytes 3145744 | tf_op jit(solution)/shard_map/all_gather | solution.py:26
  40.8 0.0 copy-done
  40.8 2.5 fusion.5
  43.3 31.1 %fusion.18 = f32[192,8192]{1,0:T(8,128)} fusion(bf16[192,4096]{1,0:T(8,128)(2,1)S(1)} %fusion.5, bf16[8192,4096]{1,0:T(8,128)(2,1)} %param.5), kind=kOutput, calls=%fused_computation.31 | convolution fusion | flops 12884901888 | bytes 74973184 | tf_op jit(solution)/shard_map/dot_general | solution.py:35
  74.5 0.0 copy-start.3
  74.5 0.0 copy-start.1
  74.5 0.0 all-reduce.6.cloned.1.call-update
  74.5 0.0 all-reduce.8.cloned.1.call-start
  74.6 0.6 copy-done.3
  75.1 0.6 dynamic-slice
  76.4 209.8 %all-reduce.6.cloned.1.call-done = f32[192,8192]{1,0:T(8,128)} async-done(((f32[192,8192]{1,0:T(8,128)}), f32[192,8192]{1,0:T(8,128)}) %all-reduce.6.cloned.1.call-update) | async-done | bytes 6291472 | tf_op jit(solution)/shard_map/psum | solution.py:39
  286.2 0.0 copy-done.1
  286.2 1.3 fusion.12
  287.5 6.9 psum.36
  294.4 0.2 dynamic-update-slice
  294.7 19.4 %all-reduce = f32[192]{0:T(256)S(1)} all-reduce(f32[192]{0:T(256)S(1)} %dynamic-update-slice), channel_id=1, replica_groups=mesh['row'=4,'col'=8] {'col'}, use_global_device_ids=true, to_apply=%add | all-reduce | flops 192 | bytes 1536
  314.1 4.0 fusion.7
  318.1 0.0 all-reduce.8.cloned.1.call-update
  318.1 0.0 all-gather.5.cloned.1.call-start
  318.1 0.5 all-gather.5.cloned.1.call-update
  318.7 0.0 all-reduce.10.cloned.1.call-start
  318.7 64.3 %all-reduce.8.cloned.1.call-done = f32[192,4096]{1,0:T(8,128)} async-done(((f32[192,4096]{1,0:T(8,128)}), f32[192,4096]{1,0:T(8,128)}) %all-reduce.8.cloned.1.call-update) | async-done | bytes 3145744 | tf_op jit(solution)/shard_map/psum | solution.py:13
  383.0 3.7 fusion.4
  386.7 30.8 %fusion.19 = f32[192,8192]{1,0:T(8,128)} fusion(bf16[192,4096]{1,0:T(8,128)(2,1)} %fusion.4, bf16[8192,4096]{1,0:T(8,128)(2,1)} %param.5), kind=kOutput, calls=%fused_computation.32 | convolution fusion | flops 12884901888 | bytes 74973184 | tf_op jit(solution)/shard_map/dot_general | solution.py:35
  417.5 0.0 all-reduce.10.cloned.1.call-update
  417.5 0.1 dynamic_slice.19
  417.6 0.0 copy-start.2
  417.6 66.8 %all-gather.5.cloned.1.call-done = bf16[2,192,8192]{2,1,0:T(8,128)(2,1)} async-done(((bf16[2,24,8192]{2,1,0:T(8,128)(2,1)}), bf16[2,192,8192]{2,1,0:T(8,128)(2,1)}) %all-gather.5.cloned.1.call-update) | async-done | bytes 6291472 | tf_op jit(solution)/shard_map/all_gather | solution.py:25
  484.4 5.4 fusion.9
  489.9 1.3 divide_bitcast_fusion
  491.1 207.2 %all-reduce.10.cloned.1.call-done = f32[192,8192]{1,0:T(8,128)} async-done(((f32[192,8192]{1,0:T(8,128)}), f32[192,8192]{1,0:T(8,128)}) %all-reduce.10.cloned.1.call-update) | async-done | bytes 6291472 | tf_op jit(solution)/shard_map/psum | solution.py:39
  698.3 0.0 copy-done.2
  698.3 1.3 fusion.11
  699.6 6.9 psum.39
  706.5 0.2 dynamic-update-slice.1
  706.7 19.4 %all-reduce.1 = f32[192]{0:T(256)S(1)} all-reduce(f32[192]{0:T(256)S(1)} %dynamic-update-slice.1), channel_id=1, replica_groups=mesh['row'=4,'col'=8] {'col'}, use_global_device_ids=true, to_apply=%add.1 | all-reduce | flops 192 | bytes 1536
  726.1 0.0 copy-start.4
  726.2 0.1 dynamic_slice.18
  726.2 1.4 divide_bitcast_fusion.1
  727.6 1.2 pad_maximum_fusion
  728.9 0.0 copy-done.4
  728.9 6.2 fusion.1
  (2 shorter events, 0.0 us)
Async XLA Ops:
  7.2 33.7 %copy-start = (bf16[96,4096]{1,0:T(8,128)(2,1)S(1)}, bf16[96,4096]{1,0:T(8,128)(2,1)}, u32[]{:S(2)}) copy-start(bf16[96,4096]{1,0:T(8,128)(2,1)} %param.6) | copy-start | bytes 2359300
  7.2 33.7 %all-gather.3.cloned.1.call-start = ((), (), s32[]{:S(2)}) async-start(), calls=%async_computation | async-start | bytes 3932160 | tf_op jit(solution)/shard_map/all_gather | solution.py:26
  7.9 278.3 %all-reduce.6.cloned.1.call-start = ((), (), s32[]{:S(2)}) async-start(), calls=%async_computation.1 | async-start | bytes 12582912 | tf_op jit(solution)/shard_map/psum | solution.py:39
  74.5 0.7 copy-start.3
  74.5 211.8 %copy-start.1 = (bf16[2,24,8192]{2,1,0:T(8,128)(2,1)S(1)}, bf16[2,24,8192]{2,1,0:T(8,128)(2,1)}, u32[]{:S(2)}) copy-start(bf16[2,24,8192]{2,1,0:T(8,128)(2,1)} %param.8) | copy-start | bytes 2359300
  74.5 308.5 %all-reduce.8.cloned.1.call-start = ((), (), s32[]{:S(2)}) async-start(), calls=%async_computation.2 | async-start | bytes 6291456 | tf_op jit(solution)/shard_map/psum | solution.py:13
  318.1 166.4 %all-gather.5.cloned.1.call-start = ((), (), s32[]{:S(2)}) async-start(), calls=%async_computation.4 | async-start | bytes 7077888 | tf_op jit(solution)/shard_map/all_gather | solution.py:25
  318.7 379.7 %all-reduce.10.cloned.1.call-start = ((), (), s32[]{:S(2)}) async-start(), calls=%async_computation.3 | async-start | bytes 12582912 | tf_op jit(solution)/shard_map/psum | solution.py:39
  417.6 280.7 %copy-start.2 = (bf16[2,24,8192]{2,1,0:T(8,128)(2,1)S(1)}, bf16[2,24,8192]{2,1,0:T(8,128)(2,1)}, u32[]{:S(2)}) copy-start(bf16[2,24,8192]{2,1,0:T(8,128)(2,1)} %param.8) | copy-start | bytes 2359300
  726.1 2.7 copy-start.4
Sparse Core Ops, SparseCore 0:
  9.6 31.2 all-gather.2
  74.6 211.5 all-reduce.5
  318.2 64.7 all-reduce.7
  385.3 99.1 all-gather.4
  488.5 209.7 all-reduce.9
where the time goes:
time: 742 us
  waiting for transfers between devices  582 us (78%)
  matrix products  79.7 us (11%)
  blocking collectives  52.5 us (7%)
  between operations  14.5 us (2%)
  other arithmetic  10.5 us (1%)
    psum x2, waiting for transfers between devices, on_device(): summed = lax.psum(partial_value, 'col')  417 us
    all_gather x1, waiting for transfers between devices, on_device(): forward_all = lax.all_gather(forward, 'col', axis=1, tiled=True)  66.8 us
    psum x1, waiting for transfers between devices, spread(): return lax.psum(kept, axis)  64.3 us
    dot_general x2, matrix products, on_device(): lax.dot_general(weighted_back, transition, (((1,), (1,)), ((), ())), pref...  61.9 us
    unnamed x2, blocking collectives  38.8 us
    all_gather x1, waiting for transfers between devices, on_device(): backward_next = lax.all_gather(backward_last, 'row', axis=0, tiled=True)  32.1 us
  transfers between devices with their start and end apart: 5, of which 5 were waited for; matrix products, arithmetic and copies ran while one was open for 6% of the time, Pallas kernels for 0%

commit v1 on v0

--- a/solution.py
+++ b/solution.py
@@ -36,7 +36,9 @@
             weighted_back, transition, (((1,), (1,)), ((), ())), preferred_element_type=jnp.float32
         )
         alpha_all = forward_all[step].astype(jnp.float32)
-        summed = lax.psum(partial_value, "col")
+        summed = partial_value
+        for hop in (1, 2, 4):
+            summed = summed + lax.ppermute(summed, "col", [(dev, dev ^ hop) for dev in range(8)])
         mine = lax.dynamic_slice_in_dim(summed, col_index * local_seqs, local_seqs, 0)
         alpha_mine = forward[step].astype(jnp.float32)
         local_norm = lax.psum(jnp.sum(alpha_mine * mine, axis=1), "row")

time: 742 us -> 1410 us (1.90)
  waiting for transfers between devices: 582 us -> 1210 us
  other arithmetic: 10.5 us -> 35 us
    ppermute x0 -> x6, waiting for transfers between devices: none -> 1120 us  [on_device(): lax.ppermute(summed, 'col', [(dev, dev ^ hop) for dev in range(8)])]
    psum x2 -> x0, waiting for transfers between devices: 417 us -> none  [on_device(): summed = lax.psum(partial_value, 'col')]
    all_gather x1, waiting for transfers between devices: 66.8 us -> 0.01 us  [on_device(): forward_all = lax.all_gather(forward, 'col', axis=1, tiled=True)]
    add x0 -> x5, other arithmetic: none -> 20.7 us  [on_device(): summed + lax.ppermute(summed, 'col', [(dev, dev ^ hop) for dev in range(8)])]
  transfers between devices with their start and end apart: 5 -> 9, of which waited for: 5 -> 8; matrix products, arithmetic and copies ran while one was open for 6% -> 1% of each run, Pallas kernels for 0% -> 0%
where the time goes in v1:
time: 1410 us
  waiting for transfers between devices  1210 us (86%)
  matrix products  78.3 us (6%)
  blocking collectives  55.3 us (4%)
  other arithmetic  35 us (2%)
  between operations  16.2 us (1%)
    ppermute x6, waiting for transfers between devices, on_device(): lax.ppermute(summed, 'col', [(dev, dev ^ hop) for dev in range(8)])  1120 us
    psum x1, waiting for transfers between devices, spread(): return lax.psum(kept, axis)  63.4 us
    dot_general x2, matrix products, on_device(): lax.dot_general(weighted_back, transition, (((1,), (1,)), ((), ())), pref...  61.8 us
    unnamed x2, blocking collectives  43.8 us
    all_gather x1, waiting for transfers between devices, on_device(): backward_next = lax.all_gather(backward_last, 'row', axis=0, tiled=True)  32.1 us
  transfers between devices with their start and end apart: 9, of which 8 were waited for; matrix products, arithmetic and copies ran while one was open for 1% of the time, Pallas kernels for 0%

profile of v1, /device:TPU:0, one launch (start us, length us, event | category | flops | bytes accessed | tf_op | source)
XLA Modules:
  0.0 1411.9 jit_solution(18185076657245575194)
XLA Ops:
  8.0 0.0 copy-start
  8.0 0.0 all-gather.3.cloned.1.call-start
  8.1 0.7 all-gather.3.cloned.1.call-update
  8.7 0.0 all-reduce.4.cloned.1.call-start
  8.8 0.8 fusion.17
  9.6 32.1 %all-gather.3.cloned.1.call-done = f32[192,4096]{1,0:T(8,128)} async-done(((f32[48,4096]{1,0:T(8,128)}), f32[192,4096]{1,0:T(8,128)}) %all-gather.3.cloned.1.call-update) | async-done | bytes 3145744 | tf_op jit(solution)/shard_map/all_gather | solution.py:26
  41.7 0.0 copy-done
  41.7 2.5 fusion.4
  44.2 31.1 %fusion.18 = f32[192,8192]{1,0:T(8,128)} fusion(bf16[192,4096]{1,0:T(8,128)(2,1)S(1)} %fusion.4, bf16[8192,4096]{1,0:T(8,128)(2,1)} %param.5), kind=kOutput, calls=%fused_computation.32 | convolution fusion | flops 12884901888 | bytes 74973184 | tf_op jit(solution)/shard_map/dot_general | solution.py:35
  75.3 1.5 collective-permute-start
  76.8 136.4 %collective-permute-done = f32[192,8192]{1,0:T(8,128)S(1)} collective-permute-done((f32[192,8192]{1,0:T(8,128)}, f32[192,8192]{1,0:T(8,128)S(1)}, u32[]{:S(2)}, u32[]{:S(2)}) %collective-permute-start) | collective-permute-done | bytes 6291488 | tf_op jit(solution)/shard_map/ppermute | solution.py:41
  213.2 3.6 add.41
  216.8 0.0 copy-start.5
  216.8 1.6 collective-permute-start.1
  218.3 135.4 %collective-permute-done.1 = f32[192,8192]{1,0:T(8,128)S(1)} collective-permute-done((f32[192,8192]{1,0:T(8,128)S(1)}, f32[192,8192]{1,0:T(8,128)S(1)}, u32[]{:S(2)}, u32[]{:S(2)}) %collective-permute-start.1) | collective-permute-done | bytes 6291488 | tf_op jit(solution)/shard_map/ppermute | solution.py:41
  353.7 3.3 add.42
  357.0 2.4 collective-permute-start.2
  359.4 0.0 copy-done.5
  359.4 0.6 dynamic-slice
  360.7 0.0 copy-start.3
  360.7 268.3 %collective-permute-done.2 = f32[192,8192]{1,0:T(8,128)} collective-permute-done((f32[192,8192]{1,0:T(8,128)}, f32[192,8192]{1,0:T(8,128)}, u32[]{:S(2)}, u32[]{:S(2)}) %collective-permute-start.2) | collective-permute-done | bytes 6291488 | tf_op jit(solution)/shard_map/ppermute | solution.py:41
  628.9 5.3 add.43
  634.2 0.0 copy-start.2
  634.3 2.6 copy-done.2
  636.9 0.0 copy-done.3
  636.9 0.2 fusion.11
  637.1 5.8 psum.21
  642.9 0.2 dynamic-update-slice
  643.1 21.5 %all-reduce = f32[192]{0:T(256)S(1)} all-reduce(f32[192]{0:T(256)S(1)} %dynamic-update-slice), channel_id=1, replica_groups=mesh['row'=4,'col'=8] {'col'}, use_global_device_ids=true, to_apply=%add | all-reduce | flops 192 | bytes 1536
  664.6 4.0 fusion.6
  668.6 0.0 all-reduce.4.cloned.1.call-update
  668.6 0.2 all-gather.5.cloned.1.call-start
  668.8 2.3 fusion.12
  671.1 63.4 %all-reduce.4.cloned.1.call-done = f32[192,4096]{1,0:T(8,128)} async-done(((f32[192,4096]{1,0:T(8,128)}), f32[192,4096]{1,0:T(8,128)}) %all-reduce.4.cloned.1.call-update) | async-done | bytes 3145744 | tf_op jit(solution)/shard_map/psum | solution.py:13
  734.5 4.4 multiply_convert_fusion
  738.9 30.7 %fusion.19 = f32[192,8192]{1,0:T(8,128)} fusion(bf16[192,4096]{1,0:T(8,128)(2,1)} %multiply_convert_fusion, bf16[8192,4096]{1,0:T(8,128)(2,1)} %param.5), kind=kOutput, calls=%fused_computation.33 | convolution fusion | flops 12884901888 | bytes 74973184 | tf_op jit(solution)/shard_map/dot_general | solution.py:35
  769.6 1.5 collective-permute-start.3
  771.0 0.0 all-gather.5.cloned.1.call-update
  771.1 178.1 %collective-permute-done.3 = f32[192,8192]{1,0:T(8,128)} collective-permute-done((f32[192,8192]{1,0:T(8,128)}, f32[192,8192]{1,0:T(8,128)}, u32[]{:S(2)}, u32[]{:S(2)}) %collective-permute-start.3) | collective-permute-done | bytes 6291488 | tf_op jit(solution)/shard_map/ppermute | solution.py:41
  949.2 5.3 add.47
  954.5 1.6 collective-permute-start.4
  956.0 134.8 %collective-permute-done.4 = f32[192,8192]{1,0:T(8,128)S(1)} collective-permute-done((f32[192,8192]{1,0:T(8,128)S(1)}, f32[192,8192]{1,0:T(8,128)S(1)}, u32[]{:S(2)}, u32[]{:S(2)}) %collective-permute-start.4) | collective-permute-done | bytes 6291488 | tf_op jit(solution)/shard_map/ppermute | solution.py:41
  1090.8 3.2 add.48
  1094.0 2.4 collective-permute-start.5
  1096.4 0.1 dynamic_slice.19
  1096.5 0.0 copy-start.4
  1096.5 0.0 all-gather.5.cloned.1.call-done
  1096.5 5.5 fusion.8
  1102.0 1.3 divide_bitcast_fusion
  1103.2 262.1 %collective-permute-done.5 = f32[192,8192]{1,0:T(8,128)} collective-permute-done((f32[192,8192]{1,0:T(8,128)}, f32[192,8192]{1,0:T(8,128)}, u32[]{:S(2)}, u32[]{:S(2)}) %collective-permute-start.5) | collective-permute-done | bytes 6291488 | tf_op jit(solution)/shard_map/ppermute | solution.py:41
  1365.4 0.0 copy-done.4
  1365.4 1.6 fusion.10
  1367.0 5.8 psum.23
  1372.8 0.2 dynamic-update-slice.1
  1373.0 22.3 %all-reduce.1 = f32[192]{0:T(256)S(1)} all-reduce(f32[192]{0:T(256)S(1)} %dynamic-update-slice.1), channel_id=1, replica_groups=mesh['row'=4,'col'=8] {'col'}, use_global_device_ids=true, to_apply=%add.1 | all-reduce | flops 192 | bytes 1536
  1395.3 0.0 copy-start.6
  1395.3 0.1 dynamic_slice.18
  1395.4 1.6 divide_bitcast_fusion.1
  1397.0 1.2 pad_maximum_fusion
  1398.3 0.0 copy-done.6
  1398.3 0.0 copy-start.1
  1398.3 6.2 fusion.1
  1404.5 0.0 copy-done.1
  (2 shorter events, 0.0 us)
Async XLA Ops:
  8.0 33.7 %copy-start = (bf16[96,4096]{1,0:T(8,128)(2,1)S(1)}, bf16[96,4096]{1,0:T(8,128)(2,1)}, u32[]{:S(2)}) copy-start(bf16[96,4096]{1,0:T(8,128)(2,1)} %param.6) | copy-start | bytes 2359300
  8.0 33.7 %all-gather.3.cloned.1.call-start = ((), (), s32[]{:S(2)}) async-start(), calls=%async_computation | async-start | bytes 3932160 | tf_op jit(solution)/shard_map/all_gather | solution.py:26
  8.7 725.7 %all-reduce.4.cloned.1.call-start = ((), (), s32[]{:S(2)}) async-start(), calls=%async_computation.1 | async-start | bytes 6291456 | tf_op jit(solution)/shard_map/psum | solution.py:13
  75.3 137.9 %collective-permute-start = (f32[192,8192]{1,0:T(8,128)}, f32[192,8192]{1,0:T(8,128)S(1)}, u32[]{:S(2)}, u32[]{:S(2)}) collective-permute-start(f32[192,8192]{1,0:T(8,128)} %fusion.18), channel_id=1, source_target_pairs={{0,1},{1,0},{2,3},{3,2},{4,5},{5,4},{6,7},{7,6},{8,9},{9,8},{10,11... | collective-permute-start | bytes 18874376 | tf_op jit(solution)/shard_map/ppermute | solution.py:41
  216.8 142.6 %copy-start.5 = (u32[32]{0:T(128)S(1)}, u32[32]{0:T(128)}, u32[]{:S(2)}) copy-start(u32[32]{0:T(128)} %constant.48) | copy-start | bytes 388
  216.8 136.9 %collective-permute-start.1 = (f32[192,8192]{1,0:T(8,128)S(1)}, f32[192,8192]{1,0:T(8,128)S(1)}, u32[]{:S(2)}, u32[]{:S(2)}) collective-permute-start(f32[192,8192]{1,0:T(8,128)S(1)} %add.41), channel_id=1, source_target_pairs={{0,2},{1,3},{2,0},{3,1},{4,6},{5,7},{6,4},{7,5},{8,10},{9,11},{10,... | collective-permute-start | bytes 18874376 | tf_op jit(solution)/shard_map/ppermute | solution.py:41
  357.0 272.0 %collective-permute-start.2 = (f32[192,8192]{1,0:T(8,128)}, f32[192,8192]{1,0:T(8,128)}, u32[]{:S(2)}, u32[]{:S(2)}) collective-permute-start(f32[192,8192]{1,0:T(8,128)} %add.42), channel_id=1, source_target_pairs={{0,4},{1,5},{2,6},{3,7},{4,0},{5,1},{6,2},{7,3},{8,12},{9,13},{10,... | collective-permute-start | bytes 18874376 | tf_op jit(solution)/shard_map/ppermute | solution.py:41
  360.7 276.2 %copy-start.3 = (bf16[2,24,8192]{2,1,0:T(8,128)(2,1)S(1)}, bf16[2,24,8192]{2,1,0:T(8,128)(2,1)}, u32[]{:S(2)}) copy-start(bf16[2,24,8192]{2,1,0:T(8,128)(2,1)} %param.8) | copy-start | bytes 2359300
  634.2 2.6 copy-start.2
  668.6 427.9 %all-gather.5.cloned.1.call-start = ((), (), s32[]{:S(2)}) async-start(), calls=%async_computation.2 | async-start | bytes 7077888 | tf_op jit(solution)/shard_map/all_gather | solution.py:25
  769.6 179.6 %collective-permute-start.3 = (f32[192,8192]{1,0:T(8,128)}, f32[192,8192]{1,0:T(8,128)}, u32[]{:S(2)}, u32[]{:S(2)}) collective-permute-start(f32[192,8192]{1,0:T(8,128)} %fusion.19), channel_id=1, source_target_pairs={{0,1},{1,0},{2,3},{3,2},{4,5},{5,4},{6,7},{7,6},{8,9},{9,8},{10,11... | collective-permute-start | bytes 18874376 | tf_op jit(solution)/shard_map/ppermute | solution.py:41
  954.5 136.3 %collective-permute-start.4 = (f32[192,8192]{1,0:T(8,128)S(1)}, f32[192,8192]{1,0:T(8,128)S(1)}, u32[]{:S(2)}, u32[]{:S(2)}) collective-permute-start(f32[192,8192]{1,0:T(8,128)S(1)} %add.47), channel_id=1, source_target_pairs={{0,2},{1,3},{2,0},{3,1},{4,6},{5,7},{6,4},{7,5},{8,10},{9,11},{10,... | collective-permute-start | bytes 18874376 | tf_op jit(solution)/shard_map/ppermute | solution.py:41
  1094.0 271.4 %collective-permute-start.5 = (f32[192,8192]{1,0:T(8,128)}, f32[192,8192]{1,0:T(8,128)}, u32[]{:S(2)}, u32[]{:S(2)}) collective-permute-start(f32[192,8192]{1,0:T(8,128)} %add.48), channel_id=1, source_target_pairs={{0,4},{1,5},{2,6},{3,7},{4,0},{5,1},{6,2},{7,3},{8,12},{9,13},{10,... | collective-permute-start | bytes 18874376 | tf_op jit(solution)/shard_map/ppermute | solution.py:41
  1096.5 268.9 %copy-start.4 = (bf16[2,24,8192]{2,1,0:T(8,128)(2,1)S(1)}, bf16[2,24,8192]{2,1,0:T(8,128)(2,1)}, u32[]{:S(2)}) copy-start(bf16[2,24,8192]{2,1,0:T(8,128)(2,1)} %param.8) | copy-start | bytes 2359300
  1395.3 3.0 copy-start.6
  1398.3 6.3 copy-start.1
Sparse Core Ops, SparseCore 0:
  10.4 31.2 all-gather.2
  668.7 65.6 all-reduce.3
Sparse Core Ops, SparseCore 1:
  771.2 135.9 all-gather.4
